TPU v7x, 32 devices: a whole 2x2x4 slice. The times are simulated.
32 devices in a mesh: groups: 2 (over y), pipe: 4 (over z), hour: 2 (over x), seg: 2 (over core).
Axes of the slice: x: 2, y: 2, z: 4, core: 2. Of those that a mesh axis runs over, the one named last changes fastest.
Arguments:
- segment_flow: float32 [16, 64, 1024], P(('groups', 'hour'), 'seg', 'pipe'), parts along dimension 0, may hold values from -4 to 4
- linepack: float32 [16, 64, 1024], P(('groups', 'hour'), 'seg', 'pipe'), parts along dimension 0, may hold values from 0.2 to 2.4
- mass_dual: float32 [16, 64, 1024], P(('groups', 'hour'), 'seg', 'pipe'), parts along dimension 0, may hold values from -3 to 3
- momentum_dual: float32 [16, 64, 1024], P(('groups', 'hour'), 'seg', 'pipe'), parts along dimension 0, may hold values from -3 to 3
- contract_dual: float32 [16, 2, 32, 128], P(('groups', 'hour'), 'seg', 'pipe'), parts along dimension 0, may hold values from -3 to 3
- flow_cost: float32 [16, 64, 1024], P(('groups', 'hour'), 'seg', 'pipe'), parts along dimension 0, may hold values from -24 to 24
- injection: float32 [16, 64, 1024], P(('groups', 'hour'), 'seg', 'pipe'), parts along dimension 0, may hold values from -3 to 3
- contract_target: float32 [16, 2, 32, 128], P(('groups', 'hour'), 'seg', 'pipe'), parts along dimension 0, may hold values from 0.4 to 2
- friction_table: float32 [16], replicated, may hold values from 0.3 to 3
- friction_class: int32 [64, 2048], P('seg', ('groups', 'pipe')), parts along dimension 1, may hold values from 0 to 15
- matching: int32 [2048], P('groups'), parts along dimension 0, may hold values from 0 to 1023, as said below
- contract_map: int32 [16, 1024], P(('groups', 'hour')), parts along dimension 0, may hold values from 0 to 127
Outputs:
- flow_final: float32 [16, 64, 1024], P(('groups', 'hour'), 'seg', 'pipe'), parts along dimension 0
- linepack_final: float32 [16, 64, 1024], P(('groups', 'hour'), 'seg', 'pipe'), parts along dimension 0
- mass_dual_final: float32 [16, 64, 1024], P(('groups', 'hour'), 'seg', 'pipe'), parts along dimension 0
- momentum_dual_final: float32 [16, 64, 1024], P(('groups', 'hour'), 'seg', 'pipe'), parts along dimension 0
- contract_dual_final: float32 [16, 2, 32, 128], P(('groups', 'hour'), 'seg', 'pipe'), parts along dimension 0
- primal_weight: float32 [2], P('groups'), parts along dimension 0
There are 2 independent parts, one for each index of `groups`. A program takes and returns all parts, laid end to end along the dimension named above; an argument that names none is the same for every part. Nothing has to cross between parts.
Inputs may be any that keep to these rules, and one draw needn't show every extreme that they name: `matching`: every pipe's inlet is fed by the outlet of exactly one pipe: each number of 0 to 1023 appears once; for any two blocks of 256 consecutive pipes, exactly 64 pipes of the first are fed from outlets of the second.
All inputs are finite; a program needn't handle non-finite values.
Results may differ from a plain program's by a relative error of at most 0.0001.
Values sent between devices are 32-bit elements; how exact they have to be, the bound alone decides.
A program may use at most 64 MiB of HBM per device.

v0:
```python
import math
import jax
import jax.numpy as jnp
from jax import lax
from jax.sharding import PartitionSpec as P

ITERS = 2
FLOW_CAP = 1.5
PACK_CAP = 2.5
STEP_SCALE = 0.25
NORM_EPS = 1e-06


def padded(cells, sides, width):
    for axis, dim in sides:
        count = lax.axis_size(axis)
        ends = count - 1
        head = lax.slice_in_dim(cells, 0, width, axis=dim)
        tail = lax.slice_in_dim(cells, cells.shape[dim] - width, cells.shape[dim], axis=dim)
        cells = jnp.concatenate(
            [
                lax.ppermute(tail, axis, [(i, (i + 1) % count) for i in range(ends)]),
                cells,
                lax.ppermute(head, axis, [((i + 1) % count, i) for i in range(ends)]),
            ],
            axis=dim,
        )
    return cells


def widened_pair(stacked):
    return padded(stacked, (("hour", 1), ("seg", 2)), 1)


def other_half(edge_row, half_index, partner_local):
    gathered = lax.all_gather(edge_row[:, None, :], ("pipe", "seg"), axis=1, tiled=True)
    hour_rows, row_count, row_width = gathered.shape
    seg_count = lax.axis_size("seg")
    picked = gathered.reshape(hour_rows, row_count // seg_count, seg_count, row_width)[
        :, :, half_index, :
    ]
    far_rows = picked.reshape(hour_rows, row_count // seg_count * row_width)
    return jnp.take(far_rows, partner_local, axis=1)


def contract_local(values, contract_rows, class_count):
    hour_rows, seg_rows, pipe_rows = values.shape
    block = math.gcd(pipe_rows, 2048)
    classes = jnp.arange(class_count, dtype=jnp.int32)

    def add_block(block_index, total):
        partial_value = lax.dynamic_slice_in_dim(values, block_index * block, block, 2)
        row_map = lax.dynamic_slice_in_dim(contract_rows, block_index * block, block, 1)
        onehot = (row_map[:, :, None] == classes[None, None, :]).astype(jnp.float32)
        return total + jnp.einsum(
            "hsp,hpc->hsc",
            partial_value,
            onehot,
            precision=lax.Precision.HIGHEST,
            preferred_element_type=jnp.float32,
        )

    return lax.fori_loop(
        0, pipe_rows // block, add_block, jnp.zeros((hour_rows, seg_rows, class_count), jnp.float32)
    )


def spread_local(duals, contract_rows):
    hour_rows, seg_rows, class_count = duals.shape
    pipe_rows = contract_rows.shape[1]
    block = math.gcd(pipe_rows, 2048)
    classes = jnp.arange(class_count, dtype=jnp.int32)

    def fill_block(block_index, result_now):
        row_map = lax.dynamic_slice_in_dim(contract_rows, block_index * block, block, 1)
        onehot = (row_map[:, :, None] == classes[None, None, :]).astype(jnp.float32)
        partial_value = jnp.einsum(
            "hsc,hpc->hsp",
            duals,
            onehot,
            precision=lax.Precision.HIGHEST,
            preferred_element_type=jnp.float32,
        )
        return lax.dynamic_update_slice_in_dim(result_now, partial_value, block_index * block, 2)

    return lax.fori_loop(
        0, pipe_rows // block, fill_block, jnp.zeros((hour_rows, seg_rows, pipe_rows), jnp.float32)
    )


def on_device(
    segment_flow,
    linepack,
    mass_dual,
    momentum_dual,
    contract_dual,
    flow_cost,
    injection,
    contract_target,
    friction_table,
    friction_class,
    matching,
    contract_map,
):
    hour_rows, seg_rows, pipe_rows = segment_flow.shape
    class_count = contract_dual.shape[3]
    pipe_count = lax.axis_size("pipe")
    total_pipes = pipe_rows * pipe_count
    share_scale = class_count / total_pipes
    pipe_start = lax.axis_index("pipe") * pipe_rows
    seg_index = lax.axis_index("seg")
    at_start = seg_index == 0
    at_end = seg_index == lax.axis_size("seg") - 1
    levels = jnp.arange(friction_table.shape[0], dtype=jnp.int32)
    friction = jnp.sum(
        jnp.where(
            friction_class[None] == levels[:, None, None], friction_table[:, None, None], 0.0
        ),
        axis=0,
    )[None]
    inverse = (
        jnp.zeros_like(matching).at[matching].set(jnp.arange(matching.shape[0], dtype=jnp.int32))
    )
    source_local = lax.dynamic_slice_in_dim(matching, pipe_start, pipe_rows)
    target_local = lax.dynamic_slice_in_dim(inverse, pipe_start, pipe_rows)
    contract_now = contract_dual.reshape(hour_rows, contract_dual.shape[2], class_count)
    target_now = contract_target.reshape(hour_rows, contract_target.shape[2], class_count)
    weight = jnp.float32(1.0)
    for iteration in range(ITERS):
        primal_step = STEP_SCALE / weight
        dual_step = STEP_SCALE * weight
        widened = widened_pair(jnp.stack([mass_dual, momentum_dual]))
        last_base = widened[0, 1:-1, -1, :]
        later_hour = widened[0, 2:, 1:-1, :]
        before_seg = widened[1, 1:-1, :-2, :]
        returned = other_half(mass_dual[:, 0, :], 0, target_local)
        last_row = last_base + jnp.where(at_end, returned, 0.0)
        next_seg = jnp.concatenate([mass_dual[:, 1:, :], last_row[:, None, :]], axis=1)
        grad_flow = mass_dual - next_seg + friction * momentum_dual
        hour_spread = spread_local(contract_now, contract_map)
        spread = lax.all_to_all(hour_spread, "pipe", split_axis=2, concat_axis=1, tiled=True)
        grad_pack = mass_dual - later_hour - momentum_dual + before_seg + share_scale * spread
        grad_flow, grad_pack = (grad_flow, grad_pack)
        flow_next = jnp.clip(
            segment_flow - primal_step * (flow_cost - grad_flow), -FLOW_CAP, FLOW_CAP
        )
        pack_next = jnp.clip(linepack + primal_step * grad_pack, 0.0, PACK_CAP)
        flow_bar = 2.0 * flow_next - segment_flow
        pack_bar = 2.0 * pack_next - linepack
        forward_widened = widened_pair(jnp.stack([flow_bar, pack_bar]))
        first_base = forward_widened[0, 1:-1, 0, :]
        earlier = forward_widened[1, :-2, 1:-1, :]
        after_seg = forward_widened[1, 1:-1, 2:, :]
        inflow = other_half(flow_bar[:, -1, :], 1, source_local)
        first_row = first_base + jnp.where(at_start, inflow, 0.0)
        upstream = jnp.concatenate([first_row[:, None, :], flow_bar[:, :-1, :]], axis=1)
        mass_rows = pack_bar - earlier + flow_bar - upstream
        momentum = friction * flow_bar - (pack_bar - after_seg)
        hour_major = lax.all_to_all(pack_bar, "pipe", split_axis=1, concat_axis=2, tiled=True)
        totals = contract_local(hour_major, contract_map, class_count)
        mass_rows, momentum, totals = (mass_rows, momentum, share_scale * totals)
        mass_next = mass_dual + dual_step * (injection - mass_rows)
        momentum_next = momentum_dual - dual_step * momentum
        contract_next = contract_now + dual_step * (target_now - totals)
        primal_sq = jnp.sum((flow_next - segment_flow) ** 2) + jnp.sum((pack_next - linepack) ** 2)
        dual_sq = (
            jnp.sum((mass_next - mass_dual) ** 2)
            + jnp.sum((momentum_next - momentum_dual) ** 2)
            + jnp.sum((contract_next - contract_now) ** 2)
        )
        primal_total, dual_total = lax.psum((primal_sq, dual_sq), ("pipe", "hour", "seg"))
        weight = jnp.sqrt(weight * jnp.sqrt((dual_total + NORM_EPS) / (primal_total + NORM_EPS)))
        segment_flow, linepack = (flow_next, pack_next)
        mass_dual, momentum_dual, contract_now = (mass_next, momentum_next, contract_next)
    return (
        segment_flow,
        linepack,
        mass_dual,
        momentum_dual,
        contract_now.reshape(contract_dual.shape),
        weight.reshape(1),
    )


def solution(mesh):
    return jax.shard_map(
        on_device,
        mesh=mesh,
        in_specs=(
            P(("groups", "hour"), "seg", "pipe"),
            P(("groups", "hour"), "seg", "pipe"),
            P(("groups", "hour"), "seg", "pipe"),
            P(("groups", "hour"), "seg", "pipe"),
            P(("groups", "hour"), "seg", "pipe", None),
            P(("groups", "hour"), "seg", "pipe"),
            P(("groups", "hour"), "seg", "pipe"),
            P(("groups", "hour"), "seg", "pipe", None),
            P(),
            P("seg", ("groups", "pipe")),
            P("groups"),
            P(("groups", "hour"), None),
        ),
        out_specs=(
            P(("groups", "hour"), "seg", "pipe"),
            P(("groups", "hour"), "seg", "pipe"),
            P(("groups", "hour"), "seg", "pipe"),
            P(("groups", "hour"), "seg", "pipe"),
            P(("groups", "hour"), "seg", "pipe", None),
            P("groups"),
        ),
        check_vma=False,
    )
```

profile of v0, /device:TPU:0, one launch (start us, length us, event | category | flops | bytes accessed | tf_op | source)
XLA Modules:
  0.0 255.9 jit_solution(9958504613072737630)
XLA Ops:
  0.6 2.2 fusion.4
  3.7 3.1 %reshape.116 = f32[4,1,8192]{2,1,0:T(1,128)} reshape(f32[1024,4,8]{2,1,0:T(4,128)S(1)} %bitcast.195) | data formatting | bytes 262144
  6.8 6.3 %all-to-all-start = ((f32[4,1,8192]{2,1,0:T(1,128)}), f32[4,1,8192]{2,1,0:T(1,128)S(1)}, u32[]{:S(2)}, u32[]{:S(2)}) async-start(f32[4,1,8192]{2,1,0:T(1,128)} %reshape.116), calls=%async_computation | async-start | bytes 262144 | tf_op jit(solution)/shard_map/all_to_all | solution.py:141
  14.5 4.5 %collective-permute-start = (f32[2,1,32,256]{3,2,1,0:T(8,128)S(1)}, f32[2,1,32,256]{3,2,1,0:T(8,128)S(1)}, u32[]{:S(2)}, u32[]{:S(2)}) collective-permute-start(f32[2,1,32,256]{3,2,1,0:T(8,128)S(1)} %get-tuple-element.135), channel_id=1, source_target_pairs={{0,2},{1,3},{4,6},{5,7},{8,10},{9,11},{12,14},{13,15},{16,18},{17,... | collective-permute-start | bytes 196616 | tf_op jit(solution)/shard_map/ppermute | solution.py:22
  19.1 14.6 %all_gather.12 = f32[4,8,256]{2,0,1:T(4,128)S(1)} all-gather(f32[4,1,256]{2,0,1:T(4,128)S(1)} %copy.255), channel_id=1, replica_groups=mesh['groups'=2,'pipe'=4,'hour'=2,'seg'=2] {'pipe','seg'}, dimensions={1}, use_global_device_ids=true | all-gather | bytes 36864 | tf_op jit(solution)/shard_map/all_gather | solution.py:36
  33.9 4.3 %scatter_custom_fusion = s32[1024]{0:T(1024)S(1)} fusion(s32[1024]{0:T(1024)S(1)} %compare_select_fusion, s32[1024]{0:T(1024)S(1)} %iota.14, s32[]{:T(128)} %constant.26.clone.1), kind=kCustom, calls=%fused_computation.140 | custom fusion | bytes 4100 | tf_op jit(solution)/shard_map/scatter | solution.py:122
  40.3 2.2 collective-permute-start.3
  47.8 2.5 reshape.117
  50.4 1.8 broadcast_multiply_fusion.1
  52.2 1.9 copy.145
  58.7 4.5 %collective-permute-start.4 = (f32[2,1,32,256]{3,2,1,0:T(8,128)S(1)}, f32[2,1,32,256]{3,2,1,0:T(8,128)S(1)}, u32[]{:S(2)}, u32[]{:S(2)}) collective-permute-start(f32[2,1,32,256]{3,2,1,0:T(8,128)S(1)} %get-tuple-element.131), channel_id=1, source_target_pairs={{0,2},{1,3},{4,6},{5,7},{8,10},{9,11},{12,14},{13,15},{16,18},{17,... | collective-permute-start | bytes 196616 | tf_op jit(solution)/shard_map/ppermute | solution.py:22
  63.3 14.0 %all_gather.13 = f32[4,8,256]{2,0,1:T(4,128)S(1)} all-gather(f32[4,1,256]{2,0,1:T(4,128)S(1)} %slice.182), channel_id=1, replica_groups=mesh['groups'=2,'pipe'=4,'hour'=2,'seg'=2] {'pipe','seg'}, dimensions={1}, use_global_device_ids=true | all-gather | bytes 36864 | tf_op jit(solution)/shard_map/all_gather | solution.py:36
  78.7 2.2 collective-permute-start.6
  84.0 2.0 multiply_reduce_fusion.7
  87.5 4.5 %collective-permute-start.8 = (f32[2,1,32,256]{3,2,1,0:T(8,128)S(1)}, f32[2,1,32,256]{3,2,1,0:T(8,128)S(1)}, u32[]{:S(2)}, u32[]{:S(2)}) collective-permute-start(f32[2,1,32,256]{3,2,1,0:T(8,128)S(1)} %get-tuple-element.127), channel_id=1, source_target_pairs={{0,2},{1,3},{4,6},{5,7},{8,10},{9,11},{12,14},{13,15},{16,18},{17,... | collective-permute-start | bytes 196616 | tf_op jit(solution)/shard_map/ppermute | solution.py:22
  92.0 4.5 %all-to-all-start.1 = ((f32[4,32,256]{2,0,1:T(4,128)}), f32[4,32,256]{2,0,1:T(4,128)S(1)}, u32[]{:S(2)}, u32[]{:S(2)}) async-start(f32[4,32,256]{2,0,1:T(4,128)} %multiply_subtract_fusion.3), calls=%async_computation.1 | async-start | bytes 262144 | tf_op jit(solution)/shard_map/all_to_all | solution.py:159
  98.5 14.6 %all_gather.14 = f32[4,8,256]{2,0,1:T(4,128)S(1)} all-gather(f32[4,1,256]{2,0,1:T(4,128)S(1)} %slice.191), channel_id=1, replica_groups=mesh['groups'=2,'pipe'=4,'hour'=2,'seg'=2] {'pipe','seg'}, dimensions={1}, use_global_device_ids=true | all-gather | bytes 36864 | tf_op jit(solution)/shard_map/all_gather | solution.py:36
  116.3 2.2 collective-permute-start.11
  120.7 2.2 fusion.73
  122.9 1.8 fusion.1
  125.6 3.1 %reshape.118 = f32[4,1,8192]{2,1,0:T(1,128)} reshape(f32[1024,4,8]{2,1,0:T(4,128)S(1)} %bitcast.197) | data formatting | bytes 262144
  128.7 4.5 %all-to-all-start.2 = ((f32[4,1,8192]{2,1,0:T(1,128)}), f32[4,1,8192]{2,1,0:T(1,128)S(1)}, u32[]{:S(2)}, u32[]{:S(2)}) async-start(f32[4,1,8192]{2,1,0:T(1,128)} %reshape.118), calls=%async_computation.2 | async-start | bytes 262144 | tf_op jit(solution)/shard_map/all_to_all | solution.py:141
  135.1 33.5 %all-reduce.1 = (f32[]{:T(128)}, f32[]{:T(128)}) all-reduce(f32[]{:T(128)S(6)} %add.153, f32[]{:T(128)S(6)} %add.155), channel_id=1, replica_groups=mesh['groups'=2,'pipe'=4,'hour'=2,'seg'=2] {'pipe','hour','seg'}, use_global_device_ids=true, to_apply=%region_5.7 | all-reduce | flops 2 | bytes 16 | tf_op jit(solution)/shard_map/psum | solution.py:171
  171.0 2.5 reshape.119
  175.4 1.9 copy.175
  181.3 4.5 %collective-permute-start.12 = (f32[2,1,32,256]{3,2,1,0:T(8,128)S(1)}, f32[2,1,32,256]{3,2,1,0:T(8,128)S(1)}, u32[]{:S(2)}, u32[]{:S(2)}) collective-permute-start(f32[2,1,32,256]{3,2,1,0:T(8,128)S(1)} %get-tuple-element.123), channel_id=1, source_target_pairs={{0,2},{1,3},{4,6},{5,7},{8,10},{9,11},{12,14},{13,15},{16,18},{17,... | collective-permute-start | bytes 196616 | tf_op jit(solution)/shard_map/ppermute | solution.py:22
  187.2 3.5 %all-to-all-start.3 = ((f32[4,32,256]{2,0,1:T(4,128)}), f32[4,32,256]{2,0,1:T(4,128)S(1)}, u32[]{:S(2)}, u32[]{:S(2)}) async-start(f32[4,32,256]{2,0,1:T(4,128)} %multiply_subtract_fusion.1), calls=%async_computation.3 | async-start | bytes 262144 | tf_op jit(solution)/shard_map/all_to_all | solution.py:159
  190.7 14.6 %all_gather.15 = f32[4,8,256]{2,0,1:T(4,128)S(1)} all-gather(f32[4,1,256]{2,0,1:T(4,128)S(1)} %slice.198), channel_id=1, replica_groups=mesh['groups'=2,'pipe'=4,'hour'=2,'seg'=2] {'pipe','seg'}, dimensions={1}, use_global_device_ids=true | all-gather | bytes 36864 | tf_op jit(solution)/shard_map/all_gather | solution.py:36
  209.4 3.0 %collective-permute-start.14 = (f32[2,6,1,256]{1,3,2,0:T(8,128)S(1)}, f32[2,6,1,256]{1,3,2,0:T(8,128)S(1)}, u32[]{:S(2)}, u32[]{:S(2)}) collective-permute-start(f32[2,6,1,256]{1,3,2,0:T(8,128)S(1)} %copy.201), channel_id=1, source_target_pairs={{0,1},{2,3},{4,5},{6,7},{8,9},{10,11},{12,13},{14,15},{16,17},{18,... | collective-permute-start | bytes 36872 | tf_op jit(solution)/shard_map/ppermute | solution.py:22
  213.8 1.8 multiply_reduce_fusion.2
  217.6 2.4 multiply_reduce_fusion.8
  221.4 32.0 %all-reduce = (f32[]{:T(128)}, f32[]{:T(128)}) all-reduce(f32[]{:T(128)S(6)} %add.167, f32[]{:T(128)S(6)} %add.169), channel_id=1, replica_groups=mesh['groups'=2,'pipe'=4,'hour'=2,'seg'=2] {'pipe','hour','seg'}, use_global_device_ids=true, to_apply=%region_12.14 | all-reduce | flops 2 | bytes 16 | tf_op jit(solution)/shard_map/psum | solution.py:171
  (151 shorter events, 40.3 us)
Async XLA Ops:
  2.8 10.3 %copy-start = (f32[4,32,256]{2,1,0:T(8,128)S(1)}, f32[4,32,256]{2,1,0:T(8,128)}, u32[]{:S(2)}) copy-start(f32[4,32,256]{2,1,0:T(8,128)} %param.16) | copy-start | bytes 393220
  2.8 10.3 %copy-start.1 = (f32[4,32,256]{2,1,0:T(8,128)S(1)}, f32[4,32,256]{2,1,0:T(8,128)}, u32[]{:S(2)}) copy-start(f32[4,32,256]{2,1,0:T(8,128)} %param.17) | copy-start | bytes 393220
  3.7 30.2 %copy-start.12 = (s32[1024]{0:T(1024)S(1)}, s32[1024]{0:T(1024)}, u32[]{:S(2)}) copy-start(s32[1024]{0:T(1024)} %param.24) | copy-start | bytes 12292
  3.7 35.3 %copy-start.11 = (s32[32,256]{1,0:T(8,128)S(1)}, s32[32,256]{1,0:T(8,128)}, u32[]{:S(2)}) copy-start(s32[32,256]{1,0:T(8,128)} %param.23) | copy-start | bytes 98308
  3.7 35.3 %copy-start.13 = (f32[16]{0:T(128)S(1)}, f32[16]{0:T(128)}, u32[]{:S(2)}) copy-start(f32[16]{0:T(128)} %param.22) | copy-start | bytes 196
  6.8 39.5 %all-to-all-start = ((f32[4,1,8192]{2,1,0:T(1,128)}), f32[4,1,8192]{2,1,0:T(1,128)S(1)}, u32[]{:S(2)}, u32[]{:S(2)}) async-start(f32[4,1,8192]{2,1,0:T(1,128)} %reshape.116), calls=%async_computation | async-start | bytes 262144 | tf_op jit(solution)/shard_map/all_to_all | solution.py:141
  13.2 26.8 %collective-permute-start.1 = (f32[2,1,32,256]{3,2,1,0:T(8,128)S(1)}, f32[2,1,32,256]{3,2,1,0:T(8,128)S(1)}, u32[]{:S(2)}, u32[]{:S(2)}) collective-permute-start(f32[2,1,32,256]{3,2,1,0:T(8,128)S(1)} %get-tuple-element.136), channel_id=1, source_target_pairs={{2,0},{3,1},{6,4},{7,5},{10,8},{11,9},{14,12},{15,13},{18,16},{19,... | collective-permute-start | bytes 196616 | tf_op jit(solution)/shard_map/ppermute | solution.py:24
  14.5 25.5 %collective-permute-start = (f32[2,1,32,256]{3,2,1,0:T(8,128)S(1)}, f32[2,1,32,256]{3,2,1,0:T(8,128)S(1)}, u32[]{:S(2)}, u32[]{:S(2)}) collective-permute-start(f32[2,1,32,256]{3,2,1,0:T(8,128)S(1)} %get-tuple-element.135), channel_id=1, source_target_pairs={{0,2},{1,3},{4,6},{5,7},{8,10},{9,11},{12,14},{13,15},{16,18},{17,... | collective-permute-start | bytes 196616 | tf_op jit(solution)/shard_map/ppermute | solution.py:22
  40.3 13.8 %collective-permute-start.3 = (f32[2,6,1,256]{3,1,2,0:T(8,128)S(1)}, f32[2,6,1,256]{3,1,2,0:T(8,128)S(1)}, u32[]{:S(2)}, u32[]{:S(2)}) collective-permute-start(f32[2,6,1,256]{3,1,2,0:T(8,128)S(1)} %slice.177), channel_id=1, source_target_pairs={{0,1},{2,3},{4,5},{6,7},{8,9},{10,11},{12,13},{14,15},{16,17},{18,... | collective-permute-start | bytes 36872 | tf_op jit(solution)/shard_map/ppermute | solution.py:22
  42.7 3.4 %collective-permute-start.2 = (f32[2,6,1,256]{1,3,2,0:T(8,128)S(1)}, f32[2,6,1,256]{1,3,2,0:T(8,128)S(1)}, u32[]{:S(2)}, u32[]{:S(2)}) collective-permute-start(f32[2,6,1,256]{1,3,2,0:T(8,128)S(1)} %copy.191), channel_id=1, source_target_pairs={{1,0},{3,2},{5,4},{7,6},{9,8},{11,10},{13,12},{15,14},{17,16},{19,... | collective-permute-start | bytes 36872 | tf_op jit(solution)/shard_map/ppermute | solution.py:24
  52.2 2.0 copy-start.8
  52.2 2.0 copy-start.9
  57.2 26.8 %copy-start.6 = (f32[4,32,256]{2,1,0:T(8,128)S(1)}, f32[4,32,256]{2,1,0:T(8,128)}, u32[]{:S(2)}) copy-start(f32[4,32,256]{2,1,0:T(8,128)} %param.20) | copy-start | bytes 393220
  57.2 21.0 %collective-permute-start.5 = (f32[2,1,32,256]{3,2,1,0:T(8,128)S(1)}, f32[2,1,32,256]{3,2,1,0:T(8,128)S(1)}, u32[]{:S(2)}, u32[]{:S(2)}) collective-permute-start(f32[2,1,32,256]{3,2,1,0:T(8,128)S(1)} %get-tuple-element.132), channel_id=1, source_target_pairs={{2,0},{3,1},{6,4},{7,5},{10,8},{11,9},{14,12},{15,13},{18,16},{19,... | collective-permute-start | bytes 196616 | tf_op jit(solution)/shard_map/ppermute | solution.py:24
  58.7 19.6 %collective-permute-start.4 = (f32[2,1,32,256]{3,2,1,0:T(8,128)S(1)}, f32[2,1,32,256]{3,2,1,0:T(8,128)S(1)}, u32[]{:S(2)}, u32[]{:S(2)}) collective-permute-start(f32[2,1,32,256]{3,2,1,0:T(8,128)S(1)} %get-tuple-element.131), channel_id=1, source_target_pairs={{0,2},{1,3},{4,6},{5,7},{8,10},{9,11},{12,14},{13,15},{16,18},{17,... | collective-permute-start | bytes 196616 | tf_op jit(solution)/shard_map/ppermute | solution.py:22
  78.7 3.7 %collective-permute-start.6 = (f32[2,6,1,256]{1,3,2,0:T(8,128)S(1)}, f32[2,6,1,256]{1,3,2,0:T(8,128)S(1)}, u32[]{:S(2)}, u32[]{:S(2)}) collective-permute-start(f32[2,6,1,256]{1,3,2,0:T(8,128)S(1)} %copy.195), channel_id=1, source_target_pairs={{0,1},{2,3},{4,5},{6,7},{8,9},{10,11},{12,13},{14,15},{16,17},{18,... | collective-permute-start | bytes 36872 | tf_op jit(solution)/shard_map/ppermute | solution.py:22
  81.0 3.1 %collective-permute-start.7 = (f32[2,6,1,256]{3,1,2,0:T(8,128)S(1)}, f32[2,6,1,256]{3,1,2,0:T(8,128)S(1)}, u32[]{:S(2)}, u32[]{:S(2)}) collective-permute-start(f32[2,6,1,256]{3,1,2,0:T(8,128)S(1)} %slice.185), channel_id=1, source_target_pairs={{1,0},{3,2},{5,4},{7,6},{9,8},{11,10},{13,12},{15,14},{17,16},{19,... | collective-permute-start | bytes 36872 | tf_op jit(solution)/shard_map/ppermute | solution.py:24
  86.1 34.6 %copy-start.14 = (f32[4,1,8,128]{3,2,1,0:T(8,128)S(1)}, f32[4,1,8,128]{3,2,1,0:T(8,128)}, u32[]{:S(2)}) copy-start(f32[4,1,8,128]{3,2,1,0:T(8,128)} %param.18) | copy-start | bytes 49156
  86.1 34.6 %copy-start.15 = (s32[4,1024]{1,0:T(4,128)S(1)}, s32[4,1024]{1,0:T(4,128)}, u32[]{:S(2)}) copy-start(s32[4,1024]{1,0:T(4,128)} %param.25) | copy-start | bytes 49156
  86.1 34.6 %copy-start.16 = (f32[4,1,8,128]{3,2,1,0:T(8,128)S(1)}, f32[4,1,8,128]{3,2,1,0:T(8,128)}, u32[]{:S(2)}) copy-start(f32[4,1,8,128]{3,2,1,0:T(8,128)} %param.21) | copy-start | bytes 49156
  86.2 29.8 %collective-permute-start.9 = (f32[2,1,32,256]{3,2,1,0:T(8,128)S(1)}, f32[2,1,32,256]{3,2,1,0:T(8,128)S(1)}, u32[]{:S(2)}, u32[]{:S(2)}) collective-permute-start(f32[2,1,32,256]{3,2,1,0:T(8,128)S(1)} %get-tuple-element.128), channel_id=1, source_target_pairs={{2,0},{3,1},{6,4},{7,5},{10,8},{11,9},{14,12},{15,13},{18,16},{19,... | collective-permute-start | bytes 196616 | tf_op jit(solution)/shard_map/ppermute | solution.py:24
  87.5 28.5 %collective-permute-start.8 = (f32[2,1,32,256]{3,2,1,0:T(8,128)S(1)}, f32[2,1,32,256]{3,2,1,0:T(8,128)S(1)}, u32[]{:S(2)}, u32[]{:S(2)}) collective-permute-start(f32[2,1,32,256]{3,2,1,0:T(8,128)S(1)} %get-tuple-element.127), channel_id=1, source_target_pairs={{0,2},{1,3},{4,6},{5,7},{8,10},{9,11},{12,14},{13,15},{16,18},{17,... | collective-permute-start | bytes 196616 | tf_op jit(solution)/shard_map/ppermute | solution.py:22
  92.0 28.6 %all-to-all-start.1 = ((f32[4,32,256]{2,0,1:T(4,128)}), f32[4,32,256]{2,0,1:T(4,128)S(1)}, u32[]{:S(2)}, u32[]{:S(2)}) async-start(f32[4,32,256]{2,0,1:T(4,128)} %multiply_subtract_fusion.3), calls=%async_computation.1 | async-start | bytes 262144 | tf_op jit(solution)/shard_map/all_to_all | solution.py:159
  116.3 61.0 %collective-permute-start.11 = (f32[2,6,1,256]{3,1,2,0:T(8,128)S(1)}, f32[2,6,1,256]{3,1,2,0:T(8,128)S(1)}, u32[]{:S(2)}, u32[]{:S(2)}) collective-permute-start(f32[2,6,1,256]{3,1,2,0:T(8,128)S(1)} %slice.193), channel_id=1, source_target_pairs={{0,1},{2,3},{4,5},{6,7},{8,9},{10,11},{12,13},{14,15},{16,17},{18,... | collective-permute-start | bytes 36872 | tf_op jit(solution)/shard_map/ppermute | solution.py:22
  119.3 13.9 %collective-permute-start.10 = (f32[2,6,1,256]{1,3,2,0:T(8,128)}, f32[2,6,1,256]{1,3,2,0:T(8,128)}, u32[]{:S(2)}, u32[]{:S(2)}) collective-permute-start(f32[2,6,1,256]{1,3,2,0:T(8,128)} %copy.197), channel_id=1, source_target_pairs={{1,0},{3,2},{5,4},{7,6},{9,8},{11,10},{13,12},{15,14},{17,16},{19,... | collective-permute-start | bytes 36872 | tf_op jit(solution)/shard_map/ppermute | solution.py:24
  128.7 41.3 %all-to-all-start.2 = ((f32[4,1,8192]{2,1,0:T(1,128)}), f32[4,1,8192]{2,1,0:T(1,128)S(1)}, u32[]{:S(2)}, u32[]{:S(2)}) async-start(f32[4,1,8192]{2,1,0:T(1,128)} %reshape.118), calls=%async_computation.2 | async-start | bytes 262144 | tf_op jit(solution)/shard_map/all_to_all | solution.py:141
  180.0 27.6 %collective-permute-start.13 = (f32[2,1,32,256]{3,2,1,0:T(8,128)S(1)}, f32[2,1,32,256]{3,2,1,0:T(8,128)S(1)}, u32[]{:S(2)}, u32[]{:S(2)}) collective-permute-start(f32[2,1,32,256]{3,2,1,0:T(8,128)S(1)} %get-tuple-element.124), channel_id=1, source_target_pairs={{2,0},{3,1},{6,4},{7,5},{10,8},{11,9},{14,12},{15,13},{18,16},{19,... | collective-permute-start | bytes 196616 | tf_op jit(solution)/shard_map/ppermute | solution.py:24
  181.3 26.3 %collective-permute-start.12 = (f32[2,1,32,256]{3,2,1,0:T(8,128)S(1)}, f32[2,1,32,256]{3,2,1,0:T(8,128)S(1)}, u32[]{:S(2)}, u32[]{:S(2)}) collective-permute-start(f32[2,1,32,256]{3,2,1,0:T(8,128)S(1)} %get-tuple-element.123), channel_id=1, source_target_pairs={{0,2},{1,3},{4,6},{5,7},{8,10},{9,11},{12,14},{13,15},{16,18},{17,... | collective-permute-start | bytes 196616 | tf_op jit(solution)/shard_map/ppermute | solution.py:22
  187.2 26.6 %copy-start.7 = (f32[4,32,256]{2,1,0:T(8,128)S(1)}, f32[4,32,256]{2,1,0:T(8,128)}, u32[]{:S(2)}) copy-start(f32[4,32,256]{2,1,0:T(8,128)} %param.20) | copy-start | bytes 393220
  187.2 30.4 %all-to-all-start.3 = ((f32[4,32,256]{2,0,1:T(4,128)}), f32[4,32,256]{2,0,1:T(4,128)S(1)}, u32[]{:S(2)}, u32[]{:S(2)}) async-start(f32[4,32,256]{2,0,1:T(4,128)} %multiply_subtract_fusion.1), calls=%async_computation.3 | async-start | bytes 262144 | tf_op jit(solution)/shard_map/all_to_all | solution.py:159
  207.9 5.8 %collective-permute-start.15 = (f32[2,6,1,256]{3,1,2,0:T(8,128)S(1)}, f32[2,6,1,256]{3,1,2,0:T(8,128)S(1)}, u32[]{:S(2)}, u32[]{:S(2)}) collective-permute-start(f32[2,6,1,256]{3,1,2,0:T(8,128)S(1)} %slice.201), channel_id=1, source_target_pairs={{1,0},{3,2},{5,4},{7,6},{9,8},{11,10},{13,12},{15,14},{17,16},{19,... | collective-permute-start | bytes 36872 | tf_op jit(solution)/shard_map/ppermute | solution.py:24
  209.4 4.2 %collective-permute-start.14 = (f32[2,6,1,256]{1,3,2,0:T(8,128)S(1)}, f32[2,6,1,256]{1,3,2,0:T(8,128)S(1)}, u32[]{:S(2)}, u32[]{:S(2)}) collective-permute-start(f32[2,6,1,256]{1,3,2,0:T(8,128)S(1)} %copy.201), channel_id=1, source_target_pairs={{0,1},{2,3},{4,5},{6,7},{8,9},{10,11},{12,13},{14,15},{16,17},{18,... | collective-permute-start | bytes 36872 | tf_op jit(solution)/shard_map/ppermute | solution.py:22
  (5 other events, 9.7 us)
where the time goes:
time: 257 us; the launch traced here: 256 us
  blocking collectives  123 us (48%)
  starting transfers between devices  57.3 us (22%)
  local copies, waits for them, and re-layouts  34.9 us (14%)
  other arithmetic  15.8 us (6%)
  between operations  12.1 us (5%)
  matrix products  8.66 us (3%)
  waiting for transfers between devices  3.97 us (2%)
    psum x2, blocking collectives, on_device(): lax.psum((primal_sq, dual_sq), ('pipe', 'hour', 'seg'))  65.5 us
    all_gather x4, blocking collectives, other_half(): lax.all_gather(edge_row[:, None, :], ('pipe', 'seg'), axis=1, tiled=True)  57.8 us
    ppermute x8, starting transfers between devices, padded(): lax.ppermute(tail, axis, [(i, (i + 1) % count) for i in range(ends)])  27.9 us
    unnamed x55, local copies, waits for them, and re-layouts  17 us
    all_to_all x2, starting transfers between devices, on_device(): lax.all_to_all(hour_spread, 'pipe', split_axis=2, concat_axis=1, tiled=True)  10.8 us
    ppermute x8, starting transfers between devices, padded(): lax.ppermute(head, axis, [((i + 1) % count, i) for i in range(ends)])  10.6 us
    all_to_all x2, starting transfers between devices, on_device(): lax.all_to_all(pack_bar, 'pipe', split_axis=1, concat_axis=2, tiled=True)  7.96 us
  transfers between devices with their start and end apart: 20, of which 3 were waited for; matrix products, arithmetic and copies ran while one was open for 16% of the time, Pallas kernels for 0%

commit v1 on v0

--- a/solution.py
+++ b/solution.py
@@ -138,7 +138,10 @@
         next_seg = jnp.concatenate([mass_dual[:, 1:, :], last_row[:, None, :]], axis=1)
         grad_flow = mass_dual - next_seg + friction * momentum_dual
         hour_spread = spread_local(contract_now, contract_map)
-        spread = lax.all_to_all(hour_spread, "pipe", split_axis=2, concat_axis=1, tiled=True)
+        size = lax.axis_size("pipe")
+        blocks = jnp.stack(jnp.split(hour_spread, size, axis=2), axis=0)
+        blocks = lax.all_to_all(blocks, "pipe", split_axis=0, concat_axis=0)
+        spread = jnp.concatenate(blocks, axis=1)
         grad_pack = mass_dual - later_hour - momentum_dual + before_seg + share_scale * spread
         grad_flow, grad_pack = (grad_flow, grad_pack)
         flow_next = jnp.clip(

time: 257 us -> 222 us (0.86)
  local copies, waits for them, and re-layouts: 34.9 us -> 11.4 us
  other arithmetic: 15.8 us -> 6.76 us
  starting transfers between devices: 57.3 us -> 50.2 us
  waiting for transfers between devices: 3.97 us -> 7.97 us
    unnamed x55 -> x37, local copies, waits for them, and re-layouts: 17 us -> 2.16 us
    ppermute x8, starting transfers between devices: 27.9 us -> 23.2 us  [padded(): lax.ppermute(tail, axis, [(i, (i + 1) % count) for i in range(ends)])]
    ppermute x8, waiting for transfers between devices: 2.83 us -> 7.35 us  [padded(): lax.ppermute(head, axis, [((i + 1) % count, i) for i in range(ends)])]
    mul x2 -> x0, local copies, waits for them, and re-layouts: 3.8 us -> none  [on_device(): share_scale * spread]
    mul x2 -> x0, other arithmetic: 3.59 us -> none  [on_device(): share_scale * spread]
  transfers between devices with their start and end apart: 20 -> 20, of which waited for: 3 -> 5; matrix products, arithmetic and copies ran while one was open for 16% -> 10% of each run, Pallas kernels for 0% -> 0%
where the time goes in v1:
time: 222 us; the launch traced here: 221 us
  blocking collectives  124 us (56%)
  starting transfers between devices  50.2 us (23%)
  between operations  11.8 us (5%)
  local copies, waits for them, and re-layouts  11.4 us (5%)
  matrix products  8.66 us (4%)
  waiting for transfers between devices  7.97 us (4%)
  other arithmetic  6.76 us (3%)
    psum x2, blocking collectives, on_device(): lax.psum((primal_sq, dual_sq), ('pipe', 'hour', 'seg'))  67 us
    all_gather x4, blocking collectives, other_half(): lax.all_gather(edge_row[:, None, :], ('pipe', 'seg'), axis=1, tiled=True)  57.4 us
    ppermute x8, starting transfers between devices, padded(): lax.ppermute(tail, axis, [(i, (i + 1) % count) for i in range(ends)])  23.2 us
    ppermute x8, starting transfers between devices, padded(): lax.ppermute(head, axis, [((i + 1) % count, i) for i in range(ends)])  10.3 us
    all_to_all x2, starting transfers between devices, on_device(): blocks = lax.all_to_all(blocks, 'pipe', split_axis=0, concat_axis=0)  9.35 us
    ppermute x8, waiting for transfers between devices, padded(): lax.ppermute(head, axis, [((i + 1) % count, i) for i in range(ends)])  7.35 us
    all_to_all x2, starting transfers between devices, on_device(): lax.all_to_all(pack_bar, 'pipe', split_axis=1, concat_axis=2, tiled=True)  7.26 us
    dot_general x2, matrix products, add_block(): jnp.einsum('hsp,hpc->hsc', partial_value, onehot, precision=lax.Precision...  4.64 us
  transfers between devices with their start and end apart: 20, of which 5 were waited for; matrix products, arithmetic and copies ran while one was open for 10% of the time, Pallas kernels for 0%

profile of v1, /device:TPU:0, one launch (start us, length us, event | category | flops | bytes accessed | tf_op | source)
XLA Modules:
  0.0 221.2 jit_solution(16382541856927222528)
XLA Ops:
  1.5 4.8 %collective-permute-start = (f32[2,1,32,256]{3,2,1,0:T(8,128)S(1)}, f32[2,1,32,256]{3,2,1,0:T(8,128)S(1)}, u32[]{:S(2)}, u32[]{:S(2)}) collective-permute-start(f32[2,1,32,256]{3,2,1,0:T(8,128)S(1)} %get-tuple-element.149), channel_id=1, source_target_pairs={{0,2},{1,3},{4,6},{5,7},{8,10},{9,11},{12,14},{13,15},{16,18},{17,... | collective-permute-start | bytes 196616 | tf_op jit(solution)/shard_map/ppermute | solution.py:22
  6.3 1.3 collective-permute-start.1
  7.6 2.2 fusion.4
  10.6 4.9 %all-to-all-start = ((f32[4,4,8,256]{3,2,1,0:T(8,128)}), f32[4,4,8,256]{3,2,1,0:T(8,128)S(1)}, u32[]{:S(2)}, u32[]{:S(2)}) async-start(f32[4,4,8,256]{3,2,1,0:T(8,128)} %pad_maximum_fusion.24), calls=%async_computation | async-start | bytes 262144 | tf_op jit(solution)/shard_map/all_to_all | solution.py:143
  15.5 4.3 %scatter_custom_fusion = s32[1024]{0:T(1024)S(1)} fusion(s32[1024]{0:T(1024)S(1)} %compare_select_fusion, s32[1024]{0:T(1024)S(1)} %iota.14, s32[]{:T(128)} %constant.26.clone.1), kind=kCustom, calls=%fused_computation.177 | custom fusion | bytes 4100 | tf_op jit(solution)/shard_map/scatter | solution.py:122
  20.3 1.3 collective-permute-start.2
  21.6 15.1 %all_gather.12 = f32[4,8,256]{2,0,1:T(4,128)S(1)} all-gather(f32[4,1,256]{2,0,1:T(4,128)S(1)} %copy.159), channel_id=1, replica_groups=mesh['groups'=2,'pipe'=4,'hour'=2,'seg'=2] {'pipe','seg'}, dimensions={1}, use_global_device_ids=true | all-gather | bytes 36864 | tf_op jit(solution)/shard_map/all_gather | solution.py:36
  37.8 2.2 collective-permute-start.3
  41.6 4.5 %collective-permute-start.4 = (f32[2,1,32,256]{3,2,1,0:T(8,128)S(1)}, f32[2,1,32,256]{3,2,1,0:T(8,128)S(1)}, u32[]{:S(2)}, u32[]{:S(2)}) collective-permute-start(f32[2,1,32,256]{3,2,1,0:T(8,128)S(1)} %get-tuple-element.145), channel_id=1, source_target_pairs={{0,2},{1,3},{4,6},{5,7},{8,10},{9,11},{12,14},{13,15},{16,18},{17,... | collective-permute-start | bytes 196616 | tf_op jit(solution)/shard_map/ppermute | solution.py:22
  46.2 1.3 collective-permute-start.5
  48.2 3.9 %all-to-all-start.1 = ((f32[4,32,256]{2,0,1:T(4,128)}), f32[4,32,256]{2,0,1:T(4,128)S(1)}, u32[]{:S(2)}, u32[]{:S(2)}) async-start(f32[4,32,256]{2,0,1:T(4,128)} %copy.144), calls=%async_computation.1 | async-start | bytes 262144 | tf_op jit(solution)/shard_map/all_to_all | solution.py:162
  52.5 1.6 collective-permute-start.6
  54.1 14.3 %all_gather.13 = f32[4,8,256]{2,0,1:T(4,128)S(1)} all-gather(f32[4,1,256]{2,0,1:T(4,128)S(1)} %copy.141), channel_id=1, replica_groups=mesh['groups'=2,'pipe'=4,'hour'=2,'seg'=2] {'pipe','seg'}, dimensions={1}, use_global_device_ids=true | all-gather | bytes 36864 | tf_op jit(solution)/shard_map/all_gather | solution.py:36
  70.8 1.5 collective-permute-done.7
  73.1 4.4 %collective-permute-start.8 = (f32[2,1,32,256]{3,2,1,0:T(8,128)S(1)}, f32[2,1,32,256]{3,2,1,0:T(8,128)S(1)}, u32[]{:S(2)}, u32[]{:S(2)}) collective-permute-start(f32[2,1,32,256]{3,2,1,0:T(8,128)S(1)} %get-tuple-element.143), channel_id=1, source_target_pairs={{0,2},{1,3},{4,6},{5,7},{8,10},{9,11},{12,14},{13,15},{16,18},{17,... | collective-permute-start | bytes 196616 | tf_op jit(solution)/shard_map/ppermute | solution.py:22
  77.5 1.3 collective-permute-start.9
  80.2 14.0 %all_gather.14 = f32[4,8,256]{2,0,1:T(4,128)S(1)} all-gather(f32[4,1,256]{2,0,1:T(4,128)S(1)} %copy.147), channel_id=1, replica_groups=mesh['groups'=2,'pipe'=4,'hour'=2,'seg'=2] {'pipe','seg'}, dimensions={1}, use_global_device_ids=true | all-gather | bytes 36864 | tf_op jit(solution)/shard_map/all_gather | solution.py:36
  96.7 1.3 collective-permute-start.10
  98.0 3.0 %collective-permute-start.11 = (f32[2,6,1,256]{3,2,1,0:T(1,128)S(1)}, f32[2,6,1,256]{3,2,1,0:T(1,128)S(1)}, u32[]{:S(2)}, u32[]{:S(2)}) collective-permute-start(f32[2,6,1,256]{3,2,1,0:T(1,128)S(1)} %get-tuple-element.133), channel_id=1, source_target_pairs={{0,1},{2,3},{4,5},{6,7},{8,9},{10,11},{12,13},{14,15},{16,17},{18,... | collective-permute-start | bytes 36872 | tf_op jit(solution)/shard_map/ppermute | solution.py:22
  101.1 2.2 %fusion.79 = (f32[]{:T(128)}, f32[4,8,128]{2,1,0:T(8,128)S(1)}) fusion(f32[4,1,8,128]{3,2,1,0:T(8,128)S(1)} %copy-done.11, f32[4,8,1024]{2,1,0:T(8,128)S(1)} %bitcast.252, s32[4,1024]{1,0:T(4,128)S(1)} %copy-done.12, f32[4,1,8,128]{3,2,1,0:T(8,128)S(1)} %copy-done.13), kind=kOutput, calls=%fused_computation.154 | convolution fusion | flops 50884608 | bytes 196612 | tf_op jit(solution)/shard_map/while/body/eval_jaxpr/hsp,hpc->hsc/dot_general | solution.py:55
  103.3 1.8 fusion.1
  105.9 4.5 %all-to-all-start.2 = ((f32[4,4,8,256]{3,2,1,0:T(8,128)}), f32[4,4,8,256]{3,2,1,0:T(8,128)S(1)}, u32[]{:S(2)}, u32[]{:S(2)}) async-start(f32[4,4,8,256]{3,2,1,0:T(8,128)} %pad_maximum_fusion.25), calls=%async_computation.2 | async-start | bytes 262144 | tf_op jit(solution)/shard_map/all_to_all | solution.py:143
  111.2 34.3 %all-reduce.1 = (f32[]{:T(128)}, f32[]{:T(128)}) all-reduce(f32[]{:T(128)S(6)} %add.153, f32[]{:T(128)S(6)} %add.155), channel_id=1, replica_groups=mesh['groups'=2,'pipe'=4,'hour'=2,'seg'=2] {'pipe','hour','seg'}, use_global_device_ids=true, to_apply=%region_5.7 | all-reduce | flops 2 | bytes 16 | tf_op jit(solution)/shard_map/psum | solution.py:174
  149.7 1.3 collective-permute-start.13
  151.8 4.1 %collective-permute-done.13 = f32[2,1,32,256]{3,2,1,0:T(8,128)S(1)} collective-permute-done((f32[2,1,32,256]{3,2,1,0:T(8,128)S(1)}, f32[2,1,32,256]{3,2,1,0:T(8,128)S(1)}, u32[]{:S(2)}, u32[]{:S(2)}) %collective-permute-start.13) | collective-permute-done | bytes 65568 | tf_op jit(solution)/shard_map/ppermute | solution.py:24
  156.1 1.3 collective-permute-start.14
  157.4 14.0 %all_gather.15 = f32[4,8,256]{2,0,1:T(4,128)S(1)} all-gather(f32[4,1,256]{2,0,1:T(4,128)S(1)} %copy.152), channel_id=1, replica_groups=mesh['groups'=2,'pipe'=4,'hour'=2,'seg'=2] {'pipe','seg'}, dimensions={1}, use_global_device_ids=true | all-gather | bytes 36864 | tf_op jit(solution)/shard_map/all_gather | solution.py:36
  172.4 3.3 %all-to-all-start.3 = ((f32[4,32,256]{2,0,1:T(4,128)}), f32[4,32,256]{2,0,1:T(4,128)S(1)}, u32[]{:S(2)}, u32[]{:S(2)}) async-start(f32[4,32,256]{2,0,1:T(4,128)} %copy.155), calls=%async_computation.3 | async-start | bytes 262144 | tf_op jit(solution)/shard_map/all_to_all | solution.py:162
  178.5 1.5 collective-permute-done.15
  180.1 1.4 multiply_reduce_fusion.2
  182.8 2.4 %multiply_reduce_fusion.8 = (f32[]{:T(128)}, f32[4,8,128]{2,1,0:T(8,128)}) fusion(f32[4,8,128]{2,1,0:T(8,128)S(1)} %get-tuple-element.160, f32[4,8,1024]{2,1,0:T(8,128)S(1)} %bitcast.251, s32[4,1024]{1,0:T(4,128)S(1)} %copy-done.12, f32[4,1,8,128]{3,2,1,0:T(8,128)S(1)} %copy-done.13, f32[]{:T(128)S(6)} %mul.150), kind=kOutput, calls=%fused_computation.155 | convolution fusion | flops 50884608 | bytes 196616 | tf_op jit(solution)/shard_map/while/body/eval_jaxpr/hsp,hpc->hsc/dot_general | solution.py:55
  185.9 32.7 %all-reduce = (f32[]{:T(128)}, f32[]{:T(128)}) all-reduce(f32[]{:T(128)S(6)} %add.167, f32[]{:T(128)S(6)} %add.169), channel_id=1, replica_groups=mesh['groups'=2,'pipe'=4,'hour'=2,'seg'=2] {'pipe','hour','seg'}, use_global_device_ids=true, to_apply=%region_12.14 | all-reduce | flops 2 | bytes 16 | tf_op jit(solution)/shard_map/psum | solution.py:174
  (111 shorter events, 17.1 us)
Async XLA Ops:
  1.5 18.7 %collective-permute-start = (f32[2,1,32,256]{3,2,1,0:T(8,128)S(1)}, f32[2,1,32,256]{3,2,1,0:T(8,128)S(1)}, u32[]{:S(2)}, u32[]{:S(2)}) collective-permute-start(f32[2,1,32,256]{3,2,1,0:T(8,128)S(1)} %get-tuple-element.149), channel_id=1, source_target_pairs={{0,2},{1,3},{4,6},{5,7},{8,10},{9,11},{12,14},{13,15},{16,18},{17,... | collective-permute-start | bytes 196616 | tf_op jit(solution)/shard_map/ppermute | solution.py:22
  6.3 13.8 %collective-permute-start.1 = (f32[2,1,32,256]{3,2,1,0:T(8,128)S(1)}, f32[2,1,32,256]{3,2,1,0:T(8,128)S(1)}, u32[]{:S(2)}, u32[]{:S(2)}) collective-permute-start(f32[2,1,32,256]{3,2,1,0:T(8,128)S(1)} %get-tuple-element.150), channel_id=1, source_target_pairs={{2,0},{3,1},{6,4},{7,5},{10,8},{11,9},{14,12},{15,13},{18,16},{19,... | collective-permute-start | bytes 196616 | tf_op jit(solution)/shard_map/ppermute | solution.py:24
  9.8 5.6 %copy-start = (f32[4,32,256]{2,1,0:T(8,128)S(1)}, f32[4,32,256]{2,1,0:T(8,128)}, u32[]{:S(2)}) copy-start(f32[4,32,256]{2,1,0:T(8,128)} %param.16) | copy-start | bytes 393220
  9.8 5.6 %copy-start.9 = (s32[1024]{0:T(1024)S(1)}, s32[1024]{0:T(1024)}, u32[]{:S(2)}) copy-start(s32[1024]{0:T(1024)} %param.24) | copy-start | bytes 12292
  9.8 10.1 %copy-start.8 = (s32[32,256]{1,0:T(8,128)S(1)}, s32[32,256]{1,0:T(8,128)}, u32[]{:S(2)}) copy-start(s32[32,256]{1,0:T(8,128)} %param.23) | copy-start | bytes 98308
  9.8 10.1 %copy-start.10 = (f32[16]{0:T(128)S(1)}, f32[16]{0:T(128)}, u32[]{:S(2)}) copy-start(f32[16]{0:T(128)} %param.22) | copy-start | bytes 196
  9.9 10.3 %copy-start.1 = (f32[4,32,256]{2,1,0:T(8,128)S(1)}, f32[4,32,256]{2,1,0:T(8,128)}, u32[]{:S(2)}) copy-start(f32[4,32,256]{2,1,0:T(8,128)} %param.17) | copy-start | bytes 393220
  10.6 30.2 %all-to-all-start = ((f32[4,4,8,256]{3,2,1,0:T(8,128)}), f32[4,4,8,256]{3,2,1,0:T(8,128)S(1)}, u32[]{:S(2)}, u32[]{:S(2)}) async-start(f32[4,4,8,256]{3,2,1,0:T(8,128)} %pad_maximum_fusion.24), calls=%async_computation | async-start | bytes 262144 | tf_op jit(solution)/shard_map/all_to_all | solution.py:143
  20.3 19.6 %collective-permute-start.2 = (f32[2,6,1,256]{1,3,2,0:T(8,128)S(1)}, f32[2,6,1,256]{1,3,2,0:T(8,128)S(1)}, u32[]{:S(2)}, u32[]{:S(2)}) collective-permute-start(f32[2,6,1,256]{1,3,2,0:T(8,128)S(1)} %copy.158), channel_id=1, source_target_pairs={{1,0},{3,2},{5,4},{7,6},{9,8},{11,10},{13,12},{15,14},{17,16},{19,... | collective-permute-start | bytes 36872 | tf_op jit(solution)/shard_map/ppermute | solution.py:24
  36.8 4.0 %copy-start.5 = (f32[4,32,256]{2,1,0:T(8,128)S(1)}, f32[4,32,256]{2,1,0:T(8,128)}, u32[]{:S(2)}) copy-start(f32[4,32,256]{2,1,0:T(8,128)} %param.15) | copy-start | bytes 393220
  36.8 4.0 %copy-start.6 = (f32[4,32,256]{2,1,0:T(8,128)S(1)}, f32[4,32,256]{2,1,0:T(8,128)}, u32[]{:S(2)}) copy-start(f32[4,32,256]{2,1,0:T(8,128)} %param.14) | copy-start | bytes 393220
  36.8 4.0 %copy-start.7 = (f32[4,32,256]{2,1,0:T(8,128)S(1)}, f32[4,32,256]{2,1,0:T(8,128)}, u32[]{:S(2)}) copy-start(f32[4,32,256]{2,1,0:T(8,128)} %param.19) | copy-start | bytes 393220
  37.8 3.0 %collective-permute-start.3 = (f32[2,6,1,256]{3,2,1,0:T(1,128)S(1)}, f32[2,6,1,256]{3,2,1,0:T(1,128)S(1)}, u32[]{:S(2)}, u32[]{:S(2)}) collective-permute-start(f32[2,6,1,256]{3,2,1,0:T(1,128)S(1)} %get-tuple-element.137), channel_id=1, source_target_pairs={{0,1},{2,3},{4,5},{6,7},{8,9},{10,11},{12,13},{14,15},{16,17},{18,... | collective-permute-start | bytes 36872 | tf_op jit(solution)/shard_map/ppermute | solution.py:22
  41.6 10.6 %collective-permute-start.4 = (f32[2,1,32,256]{3,2,1,0:T(8,128)S(1)}, f32[2,1,32,256]{3,2,1,0:T(8,128)S(1)}, u32[]{:S(2)}, u32[]{:S(2)}) collective-permute-start(f32[2,1,32,256]{3,2,1,0:T(8,128)S(1)} %get-tuple-element.145), channel_id=1, source_target_pairs={{0,2},{1,3},{4,6},{5,7},{8,10},{9,11},{12,14},{13,15},{16,18},{17,... | collective-permute-start | bytes 196616 | tf_op jit(solution)/shard_map/ppermute | solution.py:22
  46.2 6.2 %collective-permute-start.5 = (f32[2,1,32,256]{3,2,1,0:T(8,128)S(1)}, f32[2,1,32,256]{3,2,1,0:T(8,128)S(1)}, u32[]{:S(2)}, u32[]{:S(2)}) collective-permute-start(f32[2,1,32,256]{3,2,1,0:T(8,128)S(1)} %get-tuple-element.146), channel_id=1, source_target_pairs={{2,0},{3,1},{6,4},{7,5},{10,8},{11,9},{14,12},{15,13},{18,16},{19,... | collective-permute-start | bytes 196616 | tf_op jit(solution)/shard_map/ppermute | solution.py:24
  48.2 52.8 %all-to-all-start.1 = ((f32[4,32,256]{2,0,1:T(4,128)}), f32[4,32,256]{2,0,1:T(4,128)S(1)}, u32[]{:S(2)}, u32[]{:S(2)}) async-start(f32[4,32,256]{2,0,1:T(4,128)} %copy.144), calls=%async_computation.1 | async-start | bytes 262144 | tf_op jit(solution)/shard_map/all_to_all | solution.py:162
  52.5 18.1 %collective-permute-start.6 = (f32[2,6,1,256]{1,3,2,0:T(8,128)S(1)}, f32[2,6,1,256]{1,3,2,0:T(8,128)S(1)}, u32[]{:S(2)}, u32[]{:S(2)}) collective-permute-start(f32[2,6,1,256]{1,3,2,0:T(8,128)S(1)} %copy.161), channel_id=1, source_target_pairs={{0,1},{2,3},{4,5},{6,7},{8,9},{10,11},{12,13},{14,15},{16,17},{18,... | collective-permute-start | bytes 36872 | tf_op jit(solution)/shard_map/ppermute | solution.py:22
  68.3 4.0 %copy-start.2 = (f32[4,32,256]{2,1,0:T(8,128)S(1)}, f32[4,32,256]{2,1,0:T(8,128)}, u32[]{:S(2)}) copy-start(f32[4,32,256]{2,1,0:T(8,128)} %param.20) | copy-start | bytes 393220
  69.3 3.1 %collective-permute-start.7 = (f32[2,6,1,256]{3,2,1,0:T(1,128)S(1)}, f32[2,6,1,256]{3,2,1,0:T(1,128)S(1)}, u32[]{:S(2)}, u32[]{:S(2)}) collective-permute-start(f32[2,6,1,256]{3,2,1,0:T(1,128)S(1)} %get-tuple-element.136), channel_id=1, source_target_pairs={{1,0},{3,2},{5,4},{7,6},{9,8},{11,10},{13,12},{15,14},{17,16},{19,... | collective-permute-start | bytes 36872 | tf_op jit(solution)/shard_map/ppermute | solution.py:24
  73.1 23.4 %collective-permute-start.8 = (f32[2,1,32,256]{3,2,1,0:T(8,128)S(1)}, f32[2,1,32,256]{3,2,1,0:T(8,128)S(1)}, u32[]{:S(2)}, u32[]{:S(2)}) collective-permute-start(f32[2,1,32,256]{3,2,1,0:T(8,128)S(1)} %get-tuple-element.143), channel_id=1, source_target_pairs={{0,2},{1,3},{4,6},{5,7},{8,10},{9,11},{12,14},{13,15},{16,18},{17,... | collective-permute-start | bytes 196616 | tf_op jit(solution)/shard_map/ppermute | solution.py:22
  77.5 19.0 %collective-permute-start.9 = (f32[2,1,32,256]{3,2,1,0:T(8,128)S(1)}, f32[2,1,32,256]{3,2,1,0:T(8,128)S(1)}, u32[]{:S(2)}, u32[]{:S(2)}) collective-permute-start(f32[2,1,32,256]{3,2,1,0:T(8,128)S(1)} %get-tuple-element.144), channel_id=1, source_target_pairs={{2,0},{3,1},{6,4},{7,5},{10,8},{11,9},{14,12},{15,13},{18,16},{19,... | collective-permute-start | bytes 196616 | tf_op jit(solution)/shard_map/ppermute | solution.py:24
  94.4 6.7 %copy-start.11 = (f32[4,1,8,128]{3,2,1,0:T(8,128)S(1)}, f32[4,1,8,128]{3,2,1,0:T(8,128)}, u32[]{:S(2)}) copy-start(f32[4,1,8,128]{3,2,1,0:T(8,128)} %param.18) | copy-start | bytes 49156
  94.4 6.7 %copy-start.12 = (s32[4,1024]{1,0:T(4,128)S(1)}, s32[4,1024]{1,0:T(4,128)}, u32[]{:S(2)}) copy-start(s32[4,1024]{1,0:T(4,128)} %param.25) | copy-start | bytes 49156
  94.4 6.7 %copy-start.13 = (f32[4,1,8,128]{3,2,1,0:T(8,128)S(1)}, f32[4,1,8,128]{3,2,1,0:T(8,128)}, u32[]{:S(2)}) copy-start(f32[4,1,8,128]{3,2,1,0:T(8,128)} %param.21) | copy-start | bytes 49156
  96.7 13.7 %collective-permute-start.10 = (f32[2,6,1,256]{1,3,2,0:T(8,128)S(1)}, f32[2,6,1,256]{1,3,2,0:T(8,128)S(1)}, u32[]{:S(2)}, u32[]{:S(2)}) collective-permute-start(f32[2,6,1,256]{1,3,2,0:T(8,128)S(1)} %copy.163), channel_id=1, source_target_pairs={{1,0},{3,2},{5,4},{7,6},{9,8},{11,10},{13,12},{15,14},{17,16},{19,... | collective-permute-start | bytes 36872 | tf_op jit(solution)/shard_map/ppermute | solution.py:24
  98.0 49.0 %collective-permute-start.11 = (f32[2,6,1,256]{3,2,1,0:T(1,128)S(1)}, f32[2,6,1,256]{3,2,1,0:T(1,128)S(1)}, u32[]{:S(2)}, u32[]{:S(2)}) collective-permute-start(f32[2,6,1,256]{3,2,1,0:T(1,128)S(1)} %get-tuple-element.133), channel_id=1, source_target_pairs={{0,1},{2,3},{4,5},{6,7},{8,9},{10,11},{12,13},{14,15},{16,17},{18,... | collective-permute-start | bytes 36872 | tf_op jit(solution)/shard_map/ppermute | solution.py:22
  105.9 41.1 %all-to-all-start.2 = ((f32[4,4,8,256]{3,2,1,0:T(8,128)}), f32[4,4,8,256]{3,2,1,0:T(8,128)S(1)}, u32[]{:S(2)}, u32[]{:S(2)}) async-start(f32[4,4,8,256]{3,2,1,0:T(8,128)} %pad_maximum_fusion.25), calls=%async_computation.2 | async-start | bytes 262144 | tf_op jit(solution)/shard_map/all_to_all | solution.py:143
  148.4 3.4 %collective-permute-start.12 = (f32[2,1,32,256]{3,2,1,0:T(8,128)S(1)}, f32[2,1,32,256]{3,2,1,0:T(8,128)S(1)}, u32[]{:S(2)}, u32[]{:S(2)}) collective-permute-start(f32[2,1,32,256]{3,2,1,0:T(8,128)S(1)} %get-tuple-element.139), channel_id=1, source_target_pairs={{0,2},{1,3},{4,6},{5,7},{8,10},{9,11},{12,14},{13,15},{16,18},{17,... | collective-permute-start | bytes 196616 | tf_op jit(solution)/shard_map/ppermute | solution.py:22
  149.7 6.2 %collective-permute-start.13 = (f32[2,1,32,256]{3,2,1,0:T(8,128)S(1)}, f32[2,1,32,256]{3,2,1,0:T(8,128)S(1)}, u32[]{:S(2)}, u32[]{:S(2)}) collective-permute-start(f32[2,1,32,256]{3,2,1,0:T(8,128)S(1)} %get-tuple-element.140), channel_id=1, source_target_pairs={{2,0},{3,1},{6,4},{7,5},{10,8},{11,9},{14,12},{15,13},{18,16},{19,... | collective-permute-start | bytes 196616 | tf_op jit(solution)/shard_map/ppermute | solution.py:24
  156.1 22.2 %collective-permute-start.14 = (f32[2,6,1,256]{1,3,2,0:T(8,128)S(1)}, f32[2,6,1,256]{1,3,2,0:T(8,128)S(1)}, u32[]{:S(2)}, u32[]{:S(2)}) collective-permute-start(f32[2,6,1,256]{1,3,2,0:T(8,128)S(1)} %copy.165), channel_id=1, source_target_pairs={{0,1},{2,3},{4,5},{6,7},{8,9},{10,11},{12,13},{14,15},{16,17},{18,... | collective-permute-start | bytes 36872 | tf_op jit(solution)/shard_map/ppermute | solution.py:22
  172.4 10.4 %all-to-all-start.3 = ((f32[4,32,256]{2,0,1:T(4,128)}), f32[4,32,256]{2,0,1:T(4,128)S(1)}, u32[]{:S(2)}, u32[]{:S(2)}) async-start(f32[4,32,256]{2,0,1:T(4,128)} %copy.155), calls=%async_computation.3 | async-start | bytes 262144 | tf_op jit(solution)/shard_map/all_to_all | solution.py:162
  177.0 3.1 %collective-permute-start.15 = (f32[2,6,1,256]{3,2,1,0:T(1,128)S(1)}, f32[2,6,1,256]{3,2,1,0:T(1,128)S(1)}, u32[]{:S(2)}, u32[]{:S(2)}) collective-permute-start(f32[2,6,1,256]{3,2,1,0:T(1,128)S(1)} %get-tuple-element.131), channel_id=1, source_target_pairs={{1,0},{3,2},{5,4},{7,6},{9,8},{11,10},{13,12},{15,14},{17,16},{19,... | collective-permute-start | bytes 36872 | tf_op jit(solution)/shard_map/ppermute | solution.py:24
  (2 other events, 1.4 us)
